TPU v7x, 32 devices: a whole 2x2x4 slice. The times are simulated.
32 devices in a mesh: groups: 2 (over x), docs: 16 (over z, y, core).
Axes of the slice: x: 2, y: 2, z: 4, core: 2. Of those that a mesh axis runs over, the one named last changes fastest.
Arguments:
- prompt_queries: bfloat16 [4096, 8192], P(('groups', 'docs')), parts along dimension 0, may hold values from -24 to 24
- prompt_keys: bfloat16 [4096, 512], P(('groups', 'docs')), parts along dimension 0, may hold values from -6 to 6
- prompt_values: bfloat16 [4096, 512], P(('groups', 'docs')), parts along dimension 0, may hold values from -6 to 6
- cache_keys: bfloat16 [16384, 512], P(('groups', 'docs')), parts along dimension 0, may hold values from -24 to 24
- cache_values: bfloat16 [16384, 512], P(('groups', 'docs')), parts along dimension 0, may hold values from -6 to 6
- doc_blocks: int32 [16], P('groups'), parts along dimension 0, may hold values from 1 to 63, as said below
- reader_docs: int32 [32], P(('groups', 'docs')), parts along dimension 0, may hold values from 0 to 7, as said below
- reader_offsets: int32 [32], P(('groups', 'docs')), parts along dimension 0, may hold values from 0 to 4095
Outputs:
- attended: bfloat16 [4096, 8192], P(('groups', 'docs')), parts along dimension 0
There are 2 independent parts, one for each index of `groups`. A program takes and returns all parts, laid end to end along the dimension named above; each array names one. Nothing has to cross between parts.
Inputs may be any that keep to these rules, and one draw needn't show every extreme that they name: `doc_blocks`: the lengths sum to 256; the longest is exactly 63. `reader_docs`: reader r's document holds one or more of the blocks r * 16 to (r + 1) * 16 - 1.
All inputs are finite; a program needn't handle non-finite values.
Results may differ from a plain program's by a relative error of at most 0.012.
The roundings to bfloat16 on the way count: a program that leaves them out, or rounds other values in their place, can miss the bound.
Values may be sent and summed in bfloat16 or wider, within the bound.
No kernel may reach another device: no remote copies, remote signals or barrier semaphores. Data moves between devices by JAX's collectives and lax.ppermute only.
A program may use at most 128 MiB of HBM per device.

v0:
```python
import functools
import math

import jax
import jax.numpy as jnp
import numpy as np
from jax import lax
from jax.experimental import pallas as pl
from jax.experimental.pallas import tpu as pltpu
from jax.sharding import PartitionSpec as P

HD = 128
BLK = 32
HALF_KV = 2
F32 = jnp.float32
BF16 = jnp.bfloat16

rope_base = 1000000.0
yarn_factor = 4.0
pretrain_context = 32768.0
beta_fast = 32.0
beta_slow = 1.0
attention_gain = 0.1 * math.log(4.0) + 1.0
score_scale = 1.0 / math.sqrt(HD)
EXP2_SCALE = score_scale * math.log2(math.e)
SAFE_LOG2 = 64.0
masked_score = -1e30
ROW_TILE_HEADS = 4
VMEM = 56 * 1024 * 1024


def yarn_table():
    half = HD // 2

    def correction(turns):
        return (
            HD * math.log(pretrain_context / (turns * 2.0 * math.pi)) / (2.0 * math.log(rope_base))
        )

    lower = max(math.floor(correction(beta_fast)), 0)
    upper = min(math.ceil(correction(beta_slow)), HD - 1)
    span_width = max(upper - lower, 0.001)
    table = []
    for column in range(half):
        base_freq = rope_base ** (-2.0 * column / HD)
        fraction = min(max((column - lower) / span_width, 0.0), 1.0)
        table.append(base_freq * fraction / yarn_factor + base_freq * (1.0 - fraction))
    return np.asarray(table, np.float32).astype(np.float64)


def angle_rows(positions, gain):
    angles = np.asarray(positions, np.float64)[:, None] * yarn_table()[None, :]
    cosine = np.cos(angles) * gain
    sine = np.sin(angles) * gain
    return (
        np.concatenate([cosine, cosine], axis=1).astype(np.float32),
        np.concatenate([-sine, sine], axis=1).astype(np.float32),
    )


COARSE = 64


def turn(x, c1, s1, c2, s2):
    cosine = c1 * c2 - s1 * s2
    sine = s1 * c2 + c1 * s2
    return x * cosine + pltpu.roll(x, HD // 2, 1) * sine


def cache_kernel(ids, doc_blocks, bc, bs, tc, ts, k_ref, v_ref, mine_ref, theirs_ref):
    half = ids[0]
    first_block = ids[1]
    ndoc = doc_blocks.shape[0]
    width = HALF_KV * HD
    step = pl.program_id(0)
    blocks = k_ref.shape[0] // BLK
    c2 = tc[0:BLK, :]
    s2 = ts[0:BLK, :]
    for b in range(blocks):
        block = first_block + step * blocks + b

        def find(d, carry):
            start, begin = carry
            end = start + doc_blocks[d]
            return (end, jnp.where(start <= block, start, begin))

        _, begin = lax.fori_loop(0, ndoc, find, (jnp.int32(0), jnp.int32(0)), unroll=True)
        place = jnp.clip(block - begin, 0, COARSE - 1)
        c1 = bc[pl.ds(place, 1), :]
        s1 = bs[pl.ds(place, 1), :]
        cosine = c1 * c2 - s1 * s2
        sine = s1 * c2 + c1 * s2
        rows = pl.ds(b * BLK, BLK)
        for out, which in ((mine_ref, half), (theirs_ref, 1 - half)):
            for j in range(HALF_KV):
                col = pl.multiple_of(which * width + j * HD, HD)
                x = k_ref[rows, pl.ds(col, HD)].astype(F32)
                y = x * cosine + pltpu.roll(x, HD // 2, 1) * sine
                out[rows, pl.ds(j * HD, HD)] = y.astype(BF16)
    for out, which in ((mine_ref, half), (theirs_ref, 1 - half)):
        col = pl.multiple_of(which * width, HD)
        out[:, pl.ds(width, width)] = v_ref[:, pl.ds(col, width)]


def prepare_cache(ids, doc_blocks, tables, keys, values):
    tokens, columns = keys.shape
    steps = 4
    whole = lambda shape: pl.BlockSpec(shape, lambda i, *_: (0, 0))
    part = pl.BlockSpec((tokens // steps, columns), lambda i, *_: (i, 0))
    out = pl.BlockSpec((tokens // steps, columns), lambda i, *_: (i, 0))
    return pl.pallas_call(
        cache_kernel,
        grid_spec=pltpu.PrefetchScalarGridSpec(
            num_scalar_prefetch=2,
            grid=(steps,),
            in_specs=[whole(t.shape) for t in tables] + [part, part],
            out_specs=[out, out],
        ),
        out_shape=[jax.ShapeDtypeStruct((tokens, columns), BF16)] * 2,
        cost_estimate=pl.CostEstimate(flops=4000000, bytes_accessed=4 << 20, transcendentals=0),
        name="prepare_cache",
    )(ids, doc_blocks, *tables, keys, values)


def query_kernel(sel, offset, doc, ac, asn, tc, ts, q_ref, k_ref, v_ref, out_ref):
    step = pl.program_id(0)
    rows, columns = q_ref.shape
    off = jnp.clip(offset[0], 0, COARSE * COARSE - 1)
    hi = off // COARSE
    lo = off - hi * COARSE
    ca, sa = ac[pl.ds(hi, 1), :], asn[pl.ds(hi, 1), :]
    cb, sb = tc[pl.ds(lo, 1), :], ts[pl.ds(lo, 1), :]
    c1 = ca * cb - sa * sb
    s1 = sa * cb + ca * sb
    c2, s2 = tc[0:rows, :], ts[0:rows, :]
    cosine = c1 * c2 - s1 * s2
    sine = s1 * c2 + c1 * s2

    def rotated(x):
        x = x.astype(F32)
        return (x * cosine + pltpu.roll(x, HD // 2, 1) * sine).astype(BF16)

    for h in range(columns // HD):
        col = pl.multiple_of(step * columns + h * HD, HD)
        out_ref[:, pl.ds(col, HD)] = rotated(q_ref[:, h * HD : (h + 1) * HD])

    @pl.when(step == 0)
    def _():
        base = out_ref.shape[1] - (2 * HALF_KV + 1) * HD
        for j in range(HALF_KV):
            out_ref[:, base + j * HD : base + (j + 1) * HD] = rotated(
                k_ref[:, j * HD : (j + 1) * HD]
            )
        base += HALF_KV * HD
        out_ref[:, base : base + HALF_KV * HD] = v_ref[...]
        base += HALF_KV * HD
        out_ref[:, base : base + HD] = jnp.full((rows, HD), doc[0].astype(F32), F32).astype(BF16)


def prepare_queries(which, offset, doc, tables, queries, keys, values):
    rows, columns = queries.shape
    mine = columns // 2
    steps = 4
    block = mine // steps
    width = HALF_KV * HD
    whole = lambda shape: pl.BlockSpec(shape, lambda i, *_: (0, 0))
    kv = pl.BlockSpec((rows, width), lambda i, sel, *_: (0, sel[0]))
    total = mine + 2 * width + HD
    return pl.pallas_call(
        query_kernel,
        grid_spec=pltpu.PrefetchScalarGridSpec(
            num_scalar_prefetch=3,
            grid=(steps,),
            in_specs=[whole(t.shape) for t in tables]
            + [pl.BlockSpec((rows, block), lambda i, sel, *_: (0, sel[0] * steps + i)), kv, kv],
            out_specs=pl.BlockSpec((rows, total), lambda i, *_: (0, 0)),
        ),
        out_shape=jax.ShapeDtypeStruct((rows, total), BF16),
        cost_estimate=pl.CostEstimate(flops=6000000, bytes_accessed=3 << 20, transcendentals=0),
        name="prepare_queries",
    )(which, offset, doc, *tables, queries, keys, values)


def scores_of(q, k):
    return lax.dot_general(q, k, (((1,), (1,)), ((), ())), preferred_element_type=F32)


def square_bound(x):
    x = x.astype(F32)
    return jnp.max(jnp.sum(x * x, axis=1, keepdims=True))


def span_of(doc_blocks, doc):
    def find(d, carry):
        total, start, end = carry
        size = doc_blocks[d]
        start = jnp.where(d == doc, total, start)
        end = jnp.where(d == doc, total + size, end)
        return (total + size, start, end)

    zero = jnp.int32(0)
    _, start, end = lax.fori_loop(0, doc_blocks.shape[0], find, (zero, zero, zero), unroll=True)
    return start * BLK, end * BLK


def causal_mask(n):
    return lax.broadcasted_iota(jnp.int32, (n, n), 1) <= lax.broadcasted_iota(jnp.int32, (n, n), 0)


def stage_kernel(nr, npieces, first, last, nall, *refs):
    refs = list(refs)
    take = lambda n: [refs.pop(0) for _ in range(n)]
    doc_blocks, bases = take(2)
    if last:
        (all_bases,) = take(1)
    readers = [take(4) for _ in range(nr)]
    pieces = [take(2) for _ in range(npieces)]
    if not first:
        acc_in, bound_in = take(2)
    if last:
        everything = take(nall)
        outs = take(nr)
        acc_ref = refs.pop(0)
        kbuf, vbuf, peak_ref, total_ref, sem = take(5)
    else:
        acc_ref, bound_ref = take(2)
    kvh = pl.program_id(0)
    rows = readers[0][0].shape[0]
    heads = readers[0][0].shape[1] // HD
    tile = ROW_TILE_HEADS * rows
    tiles = heads // ROW_TILE_HEADS
    ones = jnp.ones((rows, HD), BF16)

    for r, (q_ref, k_ref, v_ref, d_ref) in enumerate(readers):
        document = jnp.max(d_ref[0:16, :].astype(F32)).astype(jnp.int32)
        start, end = span_of(doc_blocks, document)
        acc = acc_ref.at[r, 0]

        def q_tile(t, q_ref=q_ref):
            return jnp.concatenate(
                [
                    q_ref[:, pl.ds(pl.multiple_of((t * ROW_TILE_HEADS + g) * HD, HD), HD)]
                    for g in range(ROW_TILE_HEADS)
                ],
                axis=0,
            )

        if first:
            own_k = k_ref[...]
            own_v = jnp.concatenate([v_ref[...], ones], axis=1)
            mask = causal_mask(rows)
            mask = jnp.concatenate([mask] * ROW_TILE_HEADS, axis=0)
            bound = square_bound(own_k)

            def self_tile(t, q_most, own_k=own_k, own_v=own_v, mask=mask, acc=acc):
                q = q_tile(t)
                weights = jnp.exp2(scores_of(q, own_k) * EXP2_SCALE)
                weights = jnp.where(mask, weights, 0.0).astype(BF16)
                acc[pl.ds(pl.multiple_of(t * tile, tile), tile), :] = jnp.dot(
                    weights, own_v, preferred_element_type=F32
                )
                return jnp.maximum(q_most, square_bound(q))

            q_most = lax.fori_loop(0, tiles, self_tile, jnp.float32(0.0))
            bound_ref[r, 0, 0:8, :] = jnp.full((8, HD), bound, F32)
            bound_ref[r, 0, 8:16, :] = jnp.full((8, HD), q_most, F32)
            bounds = bound_ref
        elif last:
            acc[...] = acc_in[r, 0]
        else:
            acc[...] = acc_in[r, 0]
            bound_ref[...] = bound_in[...]

        extra = [jnp.float32(0.0)]
        for p, (kp, vp) in enumerate(pieces):
            base = bases[p]
            count = kp.shape[0]
            seen = (base < end) & (base + count > start)

            @pl.when(seen)
            def _(kp=kp, vp=vp, base=base, count=count, r=r, acc=acc, start=start, end=end):
                token = base + lax.broadcasted_iota(jnp.int32, (count, HD), 0)
                shown = (token >= start) & (token < end)
                keys = kp[...]
                values = jnp.where(shown, vp[...].astype(F32), 0.0).astype(BF16)
                values = jnp.concatenate([values, shown.astype(F32).astype(BF16)], axis=1)
                if not last:
                    bound_ref[r, 0, 0:8, :] = jnp.maximum(
                        bound_ref[r, 0, 0:8, :], square_bound(keys)
                    )

                def body(t, _):
                    weights = jnp.exp2(scores_of(q_tile(t), keys) * EXP2_SCALE).astype(BF16)
                    at = pl.ds(pl.multiple_of(t * tile, tile), tile)
                    acc[at, :] += jnp.dot(weights, values, preferred_element_type=F32)
                    return 0

                lax.fori_loop(0, tiles, body, 0)

        if last:
            out = outs[r]
            bound = jnp.max(bound_in[r, 0, 0:8, :])
            for kp, vp in pieces:
                bound = jnp.maximum(bound, square_bound(kp[...]))
            q_most = jnp.max(bound_in[r, 0, 8:16, :])
            safe = bound * q_most <= (SAFE_LOG2 / EXP2_SCALE) ** 2

            @pl.when(safe)
            def _(acc=acc, out=out):
                for h in range(heads):
                    at = slice(h * rows, (h + 1) * rows)
                    out[:, h * HD : (h + 1) * HD] = (acc[at, :HD] / acc[at, HD:]).astype(BF16)

            @pl.when(jnp.logical_not(safe))
            def _(acc=acc, out=out, q_ref=q_ref, k_ref=k_ref, v_ref=v_ref, start=start, end=end):
                def absorb(h, keys, values, shown, fresh):
                    at = pl.ds(pl.multiple_of(h * rows, rows), rows)
                    q = q_ref[:, pl.ds(pl.multiple_of(h * HD, HD), HD)]
                    s = jnp.where(shown, scores_of(q, keys) * score_scale, masked_score)
                    most = jnp.max(s, axis=1, keepdims=True)
                    if fresh:
                        peak = jnp.broadcast_to(most, (rows, HD))
                    else:
                        before = peak_ref[at, :]
                        peak = jnp.maximum(before, most)
                    w = jnp.where(shown, jnp.exp(s - peak[:, :1]), 0.0)
                    total = jnp.broadcast_to(jnp.sum(w, axis=1, keepdims=True), (rows, HD))
                    gained = jnp.dot(w.astype(BF16), values, preferred_element_type=F32)
                    if not fresh:
                        factor = jnp.exp(before - peak)
                        total = total + total_ref[at, :] * factor
                        gained = gained + acc[at, 0:HD] * factor
                    peak_ref[at, :] = peak
                    total_ref[at, :] = total
                    acc[at, 0:HD] = gained

                def own(h, _):
                    absorb(h, k_ref[...], v_ref[...], causal_mask(rows), True)
                    return 0

                lax.fori_loop(0, heads, own, 0)
                for p, piece in enumerate(everything):
                    base = all_bases[p]
                    count = piece.shape[0]

                    @pl.when((base < end) & (base + count > start))
                    def _(piece=piece, base=base, count=count):
                        kcol = pl.multiple_of(kvh * HD, HD)
                        vcol = pl.multiple_of((HALF_KV + kvh) * HD, HD)
                        for col, buf in ((kcol, kbuf), (vcol, vbuf)):
                            copy = pltpu.make_async_copy(piece.at[:, pl.ds(col, HD)], buf, sem)
                            copy.start()
                            copy.wait()
                        token = base + lax.broadcasted_iota(jnp.int32, (rows, count), 1)
                        shown = (token >= start) & (token < end)

                        def body(h, _):
                            absorb(h, kbuf[...], vbuf[...], shown, False)
                            return 0

                        lax.fori_loop(0, heads, body, 0)

                def finish(h, _):
                    at = pl.ds(pl.multiple_of(h * rows, rows), rows)
                    out[:, pl.ds(pl.multiple_of(h * HD, HD), HD)] = (
                        acc[at, 0:HD] / total_ref[at, :]
                    ).astype(BF16)
                    return 0

                lax.fori_loop(0, heads, finish, 0)


def stage(doc_blocks, messages, pieces, state, everything=None, reader0=0, name="stage"):
    nr = len(messages)
    first = state is None
    last = everything is not None
    rows, width = messages[0].shape
    mine = width - (2 * HALF_KV + 1) * HD
    group = mine // HALF_KV
    heads = group // HD
    lead = mine // HD
    smem = pl.BlockSpec(memory_space=pltpu.SMEM)
    bases = jnp.stack([b for _, b in pieces]).astype(jnp.int32)
    args = [doc_blocks, bases]
    specs = [smem, smem]
    if last:
        args.append(jnp.stack([b for _, b in everything]).astype(jnp.int32))
        specs.append(smem)
    for m in messages:
        args += [m] * 4
        specs += [
            pl.BlockSpec((rows, group), lambda k: (0, k)),
            pl.BlockSpec((rows, HD), lambda k: (0, lead + k)),
            pl.BlockSpec((rows, HD), lambda k: (0, lead + HALF_KV + k)),
            pl.BlockSpec((rows, HD), lambda k: (0, lead + 2 * HALF_KV)),
        ]
    for a, _ in pieces:
        args += [a, a]
        specs += [
            pl.BlockSpec((a.shape[0], HD), lambda k: (0, k)),
            pl.BlockSpec((a.shape[0], HD), lambda k: (0, HALF_KV + k)),
        ]
    acc_shape = (2 if not last else nr, HALF_KV, heads * rows, 2 * HD)
    acc_spec = pl.BlockSpec((nr, 1, heads * rows, 2 * HD), lambda k: (reader0, k, 0, 0))
    bound_spec = pl.BlockSpec((nr, 1, 16, HD), lambda k: (reader0, k, 0, 0))
    if not first:
        args += list(state)
        specs += [acc_spec, bound_spec]
    scratch = []
    if last:
        args += [a for a, _ in everything]
        specs += [pl.BlockSpec(memory_space=pl.ANY)] * len(everything)
        count = everything[0][0].shape[0]
        out_shape = [jax.ShapeDtypeStruct((rows, mine), BF16)] * nr
        out_specs = [pl.BlockSpec((rows, group), lambda k: (0, k))] * nr
        scratch = [
            pltpu.VMEM((nr, 1, heads * rows, 2 * HD), F32),
            pltpu.VMEM((count, HD), BF16),
            pltpu.VMEM((count, HD), BF16),
            pltpu.VMEM((heads * rows, HD), F32),
            pltpu.VMEM((heads * rows, HD), F32),
            pltpu.SemaphoreType.DMA,
        ]
    else:
        out_shape = [
            jax.ShapeDtypeStruct(acc_shape, F32),
            jax.ShapeDtypeStruct((nr, HALF_KV, 16, HD), F32),
        ]
        out_specs = [acc_spec, bound_spec]
    keys = sum(a.shape[0] for a, _ in pieces)
    return pl.pallas_call(
        functools.partial(stage_kernel, nr, len(pieces), first, last, len(everything or ())),
        grid=(HALF_KV,),
        in_specs=specs,
        out_specs=out_specs,
        out_shape=out_shape,
        scratch_shapes=scratch,
        compiler_params=pltpu.CompilerParams(vmem_limit_bytes=VMEM),
        cost_estimate=pl.CostEstimate(
            flops=int(nr * HALF_KV * heads * rows * keys * HD * 2),
            bytes_accessed=8 << 20,
            transcendentals=0,
        ),
        name=name,
    )(*args)


def shards(
    prompt_queries,
    prompt_keys,
    prompt_values,
    cache_keys,
    cache_values,
    doc_blocks,
    reader_docs,
    reader_offsets,
):
    size = lax.axis_size("docs")
    me = lax.axis_index("docs").astype(jnp.int32)
    tokens = cache_keys.shape[0]
    half = lax.rem(me, 2)
    upper = lax.rem(me // 2, 2)

    def moved(x, pairs):
        return lax.ppermute(
            x, "docs", [(i, j) for i, j in pairs if 0 <= i < size and 0 <= j < size]
        )

    everyone = range(size)
    beside = lambda x: moved(x, [(i, i ^ 1) for i in everyone])
    across = lambda x: moved(x, [(i, i ^ 2) for i in everyone])
    onward = lambda x: moved(x, [(i, i + 4) for i in everyone])
    back = lambda x: moved(x, [(i, i - 4) for i in everyone])
    relay = lambda x: moved(x, [(i, i + 4 if (i // 2) % 2 == 0 else i - 4) for i in everyone])

    block_c, block_s = angle_rows(np.arange(COARSE) * BLK, attention_gain)
    coarse_c, coarse_s = angle_rows(np.arange(COARSE) * COARSE, attention_gain)
    token_c, token_s = angle_rows(np.arange(max(prompt_queries.shape[0], COARSE)), 1.0)
    cache_tables = [jnp.asarray(t) for t in (block_c, block_s, token_c[:BLK], token_s[:BLK])]
    query_tables = [jnp.asarray(t) for t in (coarse_c, coarse_s, token_c, token_s)]

    ids = jnp.stack([half, me * (tokens // BLK)])
    mine, theirs = prepare_cache(ids, doc_blocks, cache_tables, cache_keys, cache_values)
    other = beside(theirs)
    across_a = across(mine)
    prepared = [
        prepare_queries(
            w[None], reader_offsets, reader_docs, query_tables, prompt_queries, prompt_keys, prompt_values
        )
        for w in (half, 1 - half)
    ]
    own_message = prepared[0]
    side_message = beside(prepared[1])
    onward_b = onward(other)
    back_b = back(other)
    onward_a = onward(mine)
    back_a = back(mine)
    across_b = across(other)

    at = lambda chunk: chunk * tokens
    near = [(mine, at(me)), (other, at(me ^ 1))]
    state = stage(doc_blocks, [own_message, side_message], near, None, name="near")

    far_a = relay(across_a)
    far_b = across(jnp.where(upper == 0, back_b, onward_b))
    middle = [
        (across_a, at(me ^ 2)),
        (across_b, at(me ^ 3)),
        (onward_a, at(me - 4)),
        (onward_b, at((me - 4) ^ 1)),
        (back_a, at(me + 4)),
        (back_b, at((me + 4) ^ 1)),
    ]
    state = stage(doc_blocks, [own_message, side_message], middle, state, name="middle")

    partner = jnp.where(upper == 0, me - 4, me + 4) ^ 2
    far = [(far_a, at(partner)), (far_b, at(partner ^ 1))]
    everything = near + middle + far
    (side_out,) = stage(doc_blocks, [side_message], far, state, everything, 1, name="far_side")
    (own_out,) = stage(doc_blocks, [own_message], far, state, everything, 0, name="far_own")
    side_out = beside(side_out)
    low = jnp.where(half == 0, own_out, side_out)
    high = jnp.where(half == 0, side_out, own_out)
    return jnp.concatenate([low, high], axis=1)


def solution(mesh):
    both = P(("groups", "docs"))
    wide = P(("groups", "docs"), None)
    placed = (wide, wide, wide, wide, wide, P("groups"), both, both)
    return jax.shard_map(shards, mesh=mesh, in_specs=placed, out_specs=wide, check_vma=False)
```

profile of v0, /device:TPU:23, one launch (start us, length us, event | category | flops | bytes accessed | tf_op | source)
XLA Modules:
  0.0 337.3 jit_solution(17308760694819179930)
XLA Ops:
  0.0 0.6 pad_add_fusion.1.ids
  0.6 4.3 %prepare_cache.1 = (bf16[512,512]{1,0:T(8,128)(2,1)}, bf16[512,512]{1,0:T(8,128)(2,1)}) custom-call(s32[2]{0:T(128)} %pad_add_fusion.1.ids, s32[8]{0:T(128)} %refs_0_.7, f32[64,128]{1,0:T(8,128)} %constant.49.clone.bc, f32[64,128]{1,0:T(8,128)} %constant.50.clone.bs, f32[32,128]{1,0:T(8,128)} %constant.51.clone.tc, f32[32,128]{1,0:T(8,128)} %constant.52.clone.ts, ...), custom_call_target="tpu_custom_call" | custom-call | flops 4000000 | bytes 4194304 | tf_op jit(solution)/shard_map/prepare_cache/pallas_call | solution.py:111
  4.9 0.7 collective-permute-start.2
  6.9 3.7 %prepare_queries.3 = bf16[128,4736]{1,0:T(8,128)(2,1)} custom-call(s32[1]{0:T(128)} %bitcast.12.sel, s32[1]{0:T(128)S(6)} %copy.18.offset, s32[1]{0:T(128)S(6)} %copy.17.doc, f32[64,128]{1,0:T(8,128)} %constant.53.clone.ac, f32[64,128]{1,0:T(8,128)} %constant.54.clone.asn, f32[128,128]{1,0:T(8,128)} %constant.55.clone.tc, f32[128,128]{1,0:T(8,128)} %constant.56.clone.ts, ...), custom_call_target="tpu_custom_call" | custom-call | flops 6000000 | bytes 3145728 | tf_op jit(solution)/shard_map/prepare_queries/pallas_call | solution.py:169
  10.6 0.0 collective-permute-start.6
  10.6 0.2 collective-permute-start
  10.9 0.0 collective-permute-done.2.refs_12_.refs_13_.refs_14_
  10.9 2.1 collective-permute-start.3
  12.9 3.2 collective-permute-start.4
  16.2 1.9 collective-permute-start.8
  18.2 0.7 stack.87.refs_1_
  18.8 0.7 stack.84.refs_2_
  19.5 3.7 %prepare_queries.2.refs_2_.refs_3_.refs_4_.refs_5_.refs_6_ = bf16[128,4736]{1,0:T(8,128)(2,1)} custom-call(s32[1]{0:T(128)} %bitcast.10.sel, s32[1]{0:T(128)S(6)} %copy.18.offset, s32[1]{0:T(128)S(6)} %copy.17.doc, f32[64,128]{1,0:T(8,128)} %constant.53.clone.ac, f32[64,128]{1,0:T(8,128)} %constant.54.clone.asn, f32[128,128]{1,0:T(8,128)} %constant.55.clone.tc, ...), custom_call_target="tpu_custom_call" | custom-call | flops 6000000 | bytes 3145728 | tf_op jit(solution)/shard_map/prepare_queries/pallas_call | solution.py:169
  23.2 0.6 pad_add_fusion.2.refs_1_
  23.8 0.1 collective-permute-done.refs_10_.refs_11_.refs_15_
  23.9 3.3 collective-permute-start.9
  27.2 0.0 collective-permute-done.3.refs_20_.refs_21_
  27.2 0.0 copy-start.3
  27.2 1.3 collective-permute-start.7
  28.5 0.6 pad_add_fusion.refs_1_
  29.1 0.0 collective-permute-done.4.refs_16_.refs_17_.refs_18_
  29.1 0.0 copy-start.4
  29.1 2.8 collective-permute-start.1
  31.9 0.1 broadcast_select_fusion.2
  31.9 0.0 collective-permute-done.6.refs_6_.refs_7_.refs_8_.refs_9_.refs_3_.refs_4_.refs_5_
  32.0 0.0 copy-start
  32.0 0.1 collective-permute-start.5
  32.0 1.0 copy-done
  33.0 29.8 %near.1 = (f32[2,2,2048,256]{3,2,1,0:T(8,128)}, f32[2,2,16,128]{3,2,1,0:T(8,128)}) custom-call(s32[8]{0:T(128)} %refs_0_.7, s32[2]{0:T(128)} %pad_add_fusion.2.refs_1_, bf16[128,4736]{1,0:T(8,128)(2,1)} %prepare_queries.2.refs_2_.refs_3_.refs_4_.refs_5_.refs_6_, bf16[128,4736]{1,0:T(8,128)(2,1)} %prepare_queries.2.refs_2_.refs_3_.refs_4_.refs_5_.refs_6_, ...), custom_call_target="tpu_custom_call" | custom-call | flops 2147483648 | bytes 8388608 | tf_op jit(solution)/shard_map/near/pallas_call | solution.py:431
  62.8 0.0 copy-done.3
  62.8 0.0 copy-done.4
  62.9 0.0 collective-permute-done.8.refs_14_.refs_15_.refs_17_
  62.9 0.0 collective-permute-done.9.refs_18_.refs_19_
  62.9 0.0 copy-start.5
  62.9 0.0 collective-permute-done.7.refs_12_.refs_13_.refs_16_
  62.9 0.0 copy-start.6
  62.9 0.8 copy-done.5
  63.7 0.2 copy-done.6
  63.9 15.7 %middle.1 = (f32[2,2,2048,256]{3,2,1,0:T(8,128)}, f32[2,2,16,128]{3,2,1,0:T(8,128)}) custom-call(s32[8]{0:T(128)} %refs_0_.7, s32[6]{0:T(128)} %stack.87.refs_1_, bf16[128,4736]{1,0:T(8,128)(2,1)} %prepare_queries.2.refs_2_.refs_3_.refs_4_.refs_5_.refs_6_, bf16[128,4736]{1,0:T(8,128)(2,1)} %prepare_queries.2.refs_2_.refs_3_.refs_4_.refs_5_.refs_6_, ...), custom_call_target="tpu_custom_call" | custom-call | flops 6442450944 | bytes 8388608 | tf_op jit(solution)/shard_map/middle/pallas_call | solution.py:431
  79.6 0.0 collective-permute-done.1.refs_7_.refs_8_.refs_21_
  79.6 0.0 copy-start.1
  79.6 0.0 collective-permute-done.5.refs_9_.refs_10_.refs_22_
  79.6 0.0 copy-start.2
  79.6 0.8 copy-done.1
  80.4 0.2 copy-done.2
  80.6 125.4 %far_side.1 = bf16[128,4096]{1,0:T(8,128)(2,1)} custom-call(s32[8]{0:T(128)} %refs_0_.7, s32[2]{0:T(128)} %pad_add_fusion.refs_1_, s32[10]{0:T(128)} %stack.84.refs_2_, bf16[128,4736]{1,0:T(8,128)(2,1)} %copy-done, bf16[128,4736]{1,0:T(8,128)(2,1)} %copy-done, bf16[128,4736]{1,0:T(8,128)(2,1)} %copy-done, bf16[128,4736]{1,0:T(8,128)(2,1)} %copy-done, ...), custom_call_target="tpu_custom_call" | custom-call | flops 1073741824 | bytes 8388608 | tf_op jit(solution)/shard_map/far_side/pallas_call | solution.py:431
  206.0 3.2 collective-permute-start.10
  209.2 125.2 %far_own.1 = bf16[128,4096]{1,0:T(8,128)(2,1)} custom-call(s32[8]{0:T(128)} %refs_0_.7, s32[2]{0:T(128)} %pad_add_fusion.refs_1_, s32[10]{0:T(128)} %stack.84.refs_2_, bf16[128,4736]{1,0:T(8,128)(2,1)} %prepare_queries.2.refs_2_.refs_3_.refs_4_.refs_5_.refs_6_, bf16[128,4736]{1,0:T(8,128)(2,1)} %prepare_queries.2.refs_2_.refs_3_.refs_4_.refs_5_.refs_6_, ...), custom_call_target="tpu_custom_call" | custom-call | flops 1073741824 | bytes 8388608 | tf_op jit(solution)/shard_map/far_own/pallas_call | solution.py:431
  334.4 0.0 collective-permute-done.10
  334.4 1.4 broadcast_select_fusion.1
  335.8 1.5 pad_maximum_fusion
Async XLA Ops:
  4.9 5.9 %collective-permute-start.2 = (bf16[512,512]{1,0:T(8,128)(2,1)}, bf16[512,512]{1,0:T(8,128)(2,1)}, u32[]{:S(2)}, u32[]{:S(2)}) collective-permute-start(bf16[512,512]{1,0:T(8,128)(2,1)} %get-tuple-element.12), channel_id=1, source_target_pairs={{0,1},{1,0},{2,3},{3,2},{4,5},{5,4},{6,7},{7,6},{8,9},{9,8},{10,11... | collective-permute-start | bytes 1572872 | tf_op jit(solution)/shard_map/ppermute | solution.py:465
  10.6 21.3 %collective-permute-start.6 = (bf16[128,4736]{1,0:T(8,128)(2,1)}, bf16[128,4736]{1,0:T(8,128)(2,1)S(1)}, u32[]{:S(2)}, u32[]{:S(2)}) collective-permute-start(bf16[128,4736]{1,0:T(8,128)(2,1)} %prepare_queries.3), channel_id=1, source_target_pairs={{0,1},{1,0},{2,3},{3,2},{4,5},{5,4},{6,7},{7,6},{8,9},{9,8},{10,11... | collective-permute-start | bytes 3637256 | tf_op jit(solution)/shard_map/ppermute | solution.py:465
  10.6 13.3 %collective-permute-start = (bf16[512,512]{1,0:T(8,128)(2,1)}, bf16[512,512]{1,0:T(8,128)(2,1)}, u32[]{:S(2)}, u32[]{:S(2)}) collective-permute-start(bf16[512,512]{1,0:T(8,128)(2,1)} %get-tuple-element.11.refs_10_.refs_11_.refs_13_), channel_id=1, source_target_pairs={{0,2},{1,3},{2,0},{3,1},{4,6},{5,7},{6,4},{7,5},{8,10},{9,11},{10,... | collective-permute-start | bytes 1572872 | tf_op jit(solution)/shard_map/ppermute | solution.py:465
  10.9 16.3 %collective-permute-start.3 = (bf16[512,512]{1,0:T(8,128)(2,1)}, bf16[512,512]{1,0:T(8,128)(2,1)S(1)}, u32[]{:S(2)}, u32[]{:S(2)}) collective-permute-start(bf16[512,512]{1,0:T(8,128)(2,1)} %collective-permute-done.2.refs_12_.refs_13_.refs_14_), channel_id=1, source_target_pairs={{4,0},{5,1},{6,2},{7,3},{8,4},{9,5},{10,6},{11,7},{12,8},{13,9},{1... | collective-permute-start | bytes 1572872 | tf_op jit(solution)/shard_map/ppermute | solution.py:465
  12.9 16.2 %collective-permute-start.4 = (bf16[512,512]{1,0:T(8,128)(2,1)}, bf16[512,512]{1,0:T(8,128)(2,1)S(1)}, u32[]{:S(2)}, u32[]{:S(2)}) collective-permute-start(bf16[512,512]{1,0:T(8,128)(2,1)} %collective-permute-done.2.refs_12_.refs_13_.refs_14_), channel_id=1, source_target_pairs={{0,4},{1,5},{2,6},{3,7},{4,8},{5,9},{6,10},{7,11},{8,12},{9,13},{1... | collective-permute-start | bytes 1572872 | tf_op jit(solution)/shard_map/ppermute | solution.py:465
  16.2 46.7 %collective-permute-start.8 = (bf16[512,512]{1,0:T(8,128)(2,1)}, bf16[512,512]{1,0:T(8,128)(2,1)}, u32[]{:S(2)}, u32[]{:S(2)}) collective-permute-start(bf16[512,512]{1,0:T(8,128)(2,1)} %get-tuple-element.11.refs_10_.refs_11_.refs_13_), channel_id=1, source_target_pairs={{0,4},{1,5},{2,6},{3,7},{4,8},{5,9},{6,10},{7,11},{8,12},{9,13},{1... | collective-permute-start | bytes 1572872 | tf_op jit(solution)/shard_map/ppermute | solution.py:465
  23.9 38.9 %collective-permute-start.9 = (bf16[512,512]{1,0:T(8,128)(2,1)}, bf16[512,512]{1,0:T(8,128)(2,1)S(1)}, u32[]{:S(2)}, u32[]{:S(2)}) collective-permute-start(bf16[512,512]{1,0:T(8,128)(2,1)} %get-tuple-element.11.refs_10_.refs_11_.refs_13_), channel_id=1, source_target_pairs={{4,0},{5,1},{6,2},{7,3},{8,4},{9,5},{10,6},{11,7},{12,8},{13,9},{1... | collective-permute-start | bytes 1572872 | tf_op jit(solution)/shard_map/ppermute | solution.py:465
  27.2 35.6 %copy-start.3 = (bf16[512,512]{1,0:T(8,128)(2,1)}, bf16[512,512]{1,0:T(8,128)(2,1)S(1)}, u32[]{:S(2)}) copy-start(bf16[512,512]{1,0:T(8,128)(2,1)S(1)} %collective-permute-done.3.refs_20_.refs_21_) | copy-start | bytes 1572868
  27.2 35.7 %collective-permute-start.7 = (bf16[512,512]{1,0:T(8,128)(2,1)}, bf16[512,512]{1,0:T(8,128)(2,1)S(1)}, u32[]{:S(2)}, u32[]{:S(2)}) collective-permute-start(bf16[512,512]{1,0:T(8,128)(2,1)} %collective-permute-done.2.refs_12_.refs_13_.refs_14_), channel_id=1, source_target_pairs={{0,2},{1,3},{2,0},{3,1},{4,6},{5,7},{6,4},{7,5},{8,10},{9,11},{10,... | collective-permute-start | bytes 1572872 | tf_op jit(solution)/shard_map/ppermute | solution.py:465
  29.1 33.7 %copy-start.4 = (bf16[512,512]{1,0:T(8,128)(2,1)}, bf16[512,512]{1,0:T(8,128)(2,1)S(1)}, u32[]{:S(2)}) copy-start(bf16[512,512]{1,0:T(8,128)(2,1)S(1)} %collective-permute-done.4.refs_16_.refs_17_.refs_18_) | copy-start | bytes 1572868
  29.1 50.5 %collective-permute-start.1 = (bf16[512,512]{1,0:T(8,128)(2,1)}, bf16[512,512]{1,0:T(8,128)(2,1)S(1)}, u32[]{:S(2)}, u32[]{:S(2)}) collective-permute-start(bf16[512,512]{1,0:T(8,128)(2,1)} %collective-permute-done.refs_10_.refs_11_.refs_15_), channel_id=1, source_target_pairs={{0,4},{1,5},{4,8},{5,9},{6,2},{7,3},{8,12},{9,13},{10,6},{11,7},{1... | collective-permute-start | bytes 1572872 | tf_op jit(solution)/shard_map/ppermute | solution.py:465
  32.0 1.0 copy-start
  32.0 47.6 %collective-permute-start.5 = (bf16[512,512]{1,0:T(8,128)(2,1)S(1)}, bf16[512,512]{1,0:T(8,128)(2,1)S(1)}, u32[]{:S(2)}, u32[]{:S(2)}) collective-permute-start(bf16[512,512]{1,0:T(8,128)(2,1)S(1)} %broadcast_select_fusion.2), channel_id=1, source_target_pairs={{0,2},{1,3},{2,0},{3,1},{4,6},{5,7},{6,4},{7,5},{8,10},{9,11},{10,... | collective-permute-start | bytes 1572872 | tf_op jit(solution)/shard_map/ppermute | solution.py:465
  62.9 0.8 copy-start.5
  62.9 1.0 copy-start.6
  79.6 0.8 copy-start.1
  79.6 1.0 copy-start.2
  206.0 128.4 %collective-permute-start.10 = (bf16[128,4096]{1,0:T(8,128)(2,1)}, bf16[128,4096]{1,0:T(8,128)(2,1)S(1)}, u32[]{:S(2)}, u32[]{:S(2)}) collective-permute-start(bf16[128,4096]{1,0:T(8,128)(2,1)} %far_side.1), channel_id=1, source_target_pairs={{0,1},{1,0},{2,3},{3,2},{4,5},{5,4},{6,7},{7,6},{8,9},{9,8},{10,11... | collective-permute-start | bytes 3145736 | tf_op jit(solution)/shard_map/ppermute | solution.py:465
where the time goes:
time: 339 us; the launch traced here: 337 us
  Pallas kernels  308 us (91%)
  starting transfers between devices  18.8 us (6%)
  other arithmetic  4.75 us (1%)
  local copies, waits for them, and re-layouts  4.26 us (1%)
    pallas_call x4, Pallas kernels, stage(): pl.pallas_call(functools.partial(stage_kernel, nr, len(pieces), first, la...  296 us
    ppermute x11, starting transfers between devices, moved(): lax.ppermute(x, 'docs', [(i, j) for i, j in pairs if 0 <= i < size and 0...  18.8 us
    pallas_call x2, Pallas kernels, prepare_queries(): pl.pallas_call(query_kernel, grid_spec=pltpu.PrefetchScalarGridSpec(num_s...  7.43 us
  transfers between devices with their start and end apart: 11, of which 1 were waited for; matrix products, arithmetic and copies ran while one was open for 1% of the time, Pallas kernels for 53%

commit v1 on v0

v1 whole, which is shorter than its diff:
```python
import functools
import math

import jax
import jax.numpy as jnp
import numpy as np
from jax import lax
from jax.experimental import pallas as pl
from jax.experimental.pallas import tpu as pltpu
from jax.sharding import PartitionSpec as P

HD = 128
BLK = 32
HALF_KV = 2
F32 = jnp.float32
BF16 = jnp.bfloat16

rope_base = 1000000.0
yarn_factor = 4.0
pretrain_context = 32768.0
beta_fast = 32.0
beta_slow = 1.0
attention_gain = 0.1 * math.log(4.0) + 1.0
score_scale = 1.0 / math.sqrt(HD)
EXP2_SCALE = score_scale * math.log2(math.e)
SAFE_LOG2 = 60.0
masked_score = -1e30
ROW_TILE_HEADS = 4
VMEM = 56 * 1024 * 1024


def yarn_table():
    half = HD // 2

    def correction(turns):
        return (
            HD * math.log(pretrain_context / (turns * 2.0 * math.pi)) / (2.0 * math.log(rope_base))
        )

    lower = max(math.floor(correction(beta_fast)), 0)
    upper = min(math.ceil(correction(beta_slow)), HD - 1)
    span_width = max(upper - lower, 0.001)
    table = []
    for column in range(half):
        base_freq = rope_base ** (-2.0 * column / HD)
        fraction = min(max((column - lower) / span_width, 0.0), 1.0)
        table.append(base_freq * fraction / yarn_factor + base_freq * (1.0 - fraction))
    return np.asarray(table, np.float32).astype(np.float64)


def angle_rows(positions, gain):
    angles = np.asarray(positions, np.float64)[:, None] * yarn_table()[None, :]
    cosine = np.cos(angles) * gain
    sine = np.sin(angles) * gain
    return (
        np.concatenate([cosine, cosine], axis=1).astype(np.float32),
        np.concatenate([-sine, sine], axis=1).astype(np.float32),
    )


COARSE = 64


def cache_kernel(ids, doc_blocks, table, k_ref, v_ref, mine_ref, theirs_ref):
    half = ids[0]
    first_block = ids[1]
    ndoc = doc_blocks.shape[0]
    width = HALF_KV * HD
    step = pl.program_id(0)
    blocks = k_ref.shape[0] // BLK
    c2 = table[2 * COARSE : 2 * COARSE + BLK, :]
    s2 = table[2 * COARSE + BLK : 2 * COARSE + 2 * BLK, :]
    for b in range(blocks):
        block = first_block + step * blocks + b

        def find(d, carry):
            start, begin = carry
            end = start + doc_blocks[d]
            return (end, jnp.where(start <= block, start, begin))

        _, begin = lax.fori_loop(0, ndoc, find, (jnp.int32(0), jnp.int32(0)), unroll=True)
        place = jnp.clip(block - begin, 0, COARSE - 1)
        c1 = table[pl.ds(place, 1), :]
        s1 = table[pl.ds(place + COARSE, 1), :]
        cosine = c1 * c2 - s1 * s2
        sine = s1 * c2 + c1 * s2
        rows = pl.ds(b * BLK, BLK)
        for out, which in ((mine_ref, half), (theirs_ref, 1 - half)):
            for j in range(HALF_KV):
                col = pl.multiple_of(which * width + j * HD, HD)
                x = k_ref[rows, pl.ds(col, HD)].astype(F32)
                y = x * cosine + pltpu.roll(x, HD // 2, 1) * sine
                out[rows, pl.ds(j * HD, HD)] = y.astype(BF16)
    for out, which in ((mine_ref, half), (theirs_ref, 1 - half)):
        col = pl.multiple_of(which * width, HD)
        out[:, pl.ds(width, width)] = v_ref[:, pl.ds(col, width)]


def prepare_cache(ids, doc_blocks, table, keys, values):
    tokens, columns = keys.shape
    steps = 2
    whole = lambda shape: pl.BlockSpec(shape, lambda i, *_: (0, 0))
    part = pl.BlockSpec((tokens // steps, columns), lambda i, *_: (i, 0))
    out = pl.BlockSpec((tokens // steps, columns), lambda i, *_: (i, 0))
    return pl.pallas_call(
        cache_kernel,
        grid_spec=pltpu.PrefetchScalarGridSpec(
            num_scalar_prefetch=2,
            grid=(steps,),
            in_specs=[whole(table.shape), part, part],
            out_specs=[out, out],
        ),
        out_shape=[jax.ShapeDtypeStruct((tokens, columns), BF16)] * 2,
        cost_estimate=pl.CostEstimate(flops=4000000, bytes_accessed=4 << 20, transcendentals=0),
        name="prepare_cache",
    )(ids, doc_blocks, table, keys, values)


def scores_of(q, k):
    return lax.dot_general(q, k, (((1,), (1,)), ((), ())), preferred_element_type=F32)


def square_bound(x):
    x = x.astype(F32)
    sums = jnp.dot((x * x).astype(BF16), jnp.ones((HD, HD), BF16), preferred_element_type=F32)
    return jnp.max(sums.reshape(-1, 8, HD), axis=0)


def span_of(doc_blocks, doc):
    def find(d, carry):
        total, start, end = carry
        size = doc_blocks[d]
        start = jnp.where(d == doc, total, start)
        end = jnp.where(d == doc, total + size, end)
        return (total + size, start, end)

    zero = jnp.int32(0)
    _, start, end = lax.fori_loop(0, doc_blocks.shape[0], find, (zero, zero, zero), unroll=True)
    return start * BLK, end * BLK


def causal_mask(n):
    return lax.broadcasted_iota(jnp.int32, (n, n), 1) <= lax.broadcasted_iota(jnp.int32, (n, n), 0)


def whole_number(ref, place):
    return jnp.max(ref[16 * place : 16 * place + 16, :].astype(F32)).astype(jnp.int32)


def turning(table, offset_hi, offset_lo, rows):
    ca, sa = table[pl.ds(offset_hi, 1), :], table[pl.ds(offset_hi + COARSE, 1), :]
    cb = table[pl.ds(offset_lo + 2 * COARSE, 1), :]
    sb = table[pl.ds(offset_lo + 2 * COARSE + rows, 1), :]
    c1 = ca * cb - sa * sb
    s1 = sa * cb + ca * sb
    c2 = table[2 * COARSE : 2 * COARSE + rows, :]
    s2 = table[2 * COARSE + rows : 2 * COARSE + 2 * rows, :]
    return c1 * c2 - s1 * s2, s1 * c2 + c1 * s2


def stage_kernel(chunks, all_chunks, slots, count, first, last, reader0, *refs):
    refs = list(refs)
    take = lambda n: [refs.pop(0) for _ in range(n)]
    (ids,) = take(1)
    if first:
        doc_blocks, own_doc, own_offset, table = take(4)
        readers = [take(3) for _ in range(2)]
        (numbers,) = take(1)
    else:
        spans, q_ref, k_ref, v_ref = take(4)
    pieces = [take(2) for _ in chunks]
    if not first:
        acc_in, bound_in = take(2)
    if last:
        everything = take(len(slots))
        out, acc = take(2)
        most_ref, fetched_k, fetched_v, peak_ref, total_ref, sem = take(6)
    elif first:
        acc_ref, bound_ref, spans, q_ref, k_ref, v_ref = take(6)
    else:
        acc_ref, bound_ref = take(2)
    kbuf, vbuf = take(2)
    kvh = pl.program_id(0)
    reader = reader0 if last else pl.program_id(1)
    me = ids[2]
    if last:
        most = most_ref
    else:
        acc = acc_ref.at[0, 0]
        most = bound_ref.at[0, 0, 0:8]
    q_rows = q_ref.at[0, 0]
    k_own, v_own = k_ref.at[0, 0], v_ref.at[0, 0]
    rows = k_own.shape[0]
    heads = q_rows.shape[0] // rows
    tile = ROW_TILE_HEADS * rows
    tiles = heads // ROW_TILE_HEADS
    at = lambda t: slice(t * tile, (t + 1) * tile)

    if first:
        for r, (raw_q, raw_k, raw_v) in enumerate(readers):

            @pl.when(reader == r)
            def _(r=r, raw_q=raw_q, raw_k=raw_k, raw_v=raw_v):
                if r == 0:
                    document = own_doc[0]
                    offset = jnp.clip(own_offset[0], 0, COARSE * COARSE - 1)
                    hi = offset // COARSE
                    lo = offset - hi * COARSE
                else:
                    document, hi, lo = [whole_number(numbers, i) for i in range(3)]
                begin, finish = span_of(doc_blocks, document)
                spans[2 * r] = begin
                spans[2 * r + 1] = finish
                cosine, sine = turning(table, hi, lo, rows)

                def rotated(x):
                    x = x.astype(F32)
                    return (x * cosine + pltpu.roll(x, HD // 2, 1) * sine).astype(BF16)

                k_own[...] = rotated(raw_k[...])
                v_own[...] = raw_v[...]
                for h in range(heads):
                    q_rows[h * rows : (h + 1) * rows, :] = rotated(
                        raw_q[:, h * HD : (h + 1) * HD]
                    )

    start = spans[2 * reader]
    end = spans[2 * reader + 1]

    if first:
        mask = jnp.concatenate([causal_mask(rows)] * ROW_TILE_HEADS, axis=0)
        keys = k_own[...]
        values = jnp.concatenate([v_own[...], jnp.ones((rows, HD), BF16)], axis=1)
        q_most = jnp.zeros((8, HD), F32)
        for t in range(tiles):
            q = q_rows[at(t), :]
            weights = jnp.exp2(scores_of(q, keys) * EXP2_SCALE)
            weights = jnp.where(mask, weights, 0.0).astype(BF16)
            acc[at(t), :] = jnp.dot(weights, values, preferred_element_type=F32)
            q_most = jnp.maximum(q_most, square_bound(q))
        most[...] = square_bound(keys)
        bound_ref[0, 0, 8:16, :] = q_most
    elif last:
        most[...] = bound_in[0, 0, 0:8, :]
    else:
        bound_ref[...] = bound_in[...]

    filled = jnp.int32(0)
    for p in range(0, len(pieces), 2):
        bases = [chunks[p + i](me) * count for i in range(2)]
        lows = [jnp.maximum(base, start) for base in bases]
        shown = [
            jnp.maximum(jnp.minimum(base + count, end) - low, 0)
            for base, low in zip(bases, lows, strict=True)
        ]
        ahead = [jnp.where(bases[i] > bases[1 - i], shown[1 - i], 0) for i in range(2)]
        for i in range(2):

            @pl.when(shown[i] > 0)
            def _(piece=pieces[p + i], put=count + filled + ahead[i] + bases[i] - lows[i]):
                to = pl.ds(pl.multiple_of(put, BLK), count)
                kbuf[to, :] = piece[0][...]
                vbuf[to, 0:HD] = piece[1][...]
                vbuf[to, HD:] = jnp.ones((count, HD), BF16)

        filled = filled + shown[0] + shown[1]
    some = filled > 0

    @pl.when(some)
    def _():
        to = pl.ds(pl.multiple_of(count + filled, BLK), count)
        kbuf[to, :] = jnp.zeros((count, HD), BF16)
        vbuf[to, :] = jnp.zeros((count, 2 * HD), BF16)
        if not first:
            acc[...] = acc_in[0, 0]

    def attend(step, _):
        here = pl.ds(pl.multiple_of(count + step * count, BLK), count)
        keys = kbuf[here, :]
        values = vbuf[here, :]
        most[...] = jnp.maximum(most[...], square_bound(keys))
        for t in range(tiles):
            weights = jnp.exp2(scores_of(q_rows[at(t), :], keys) * EXP2_SCALE).astype(BF16)
            acc[at(t), :] += jnp.dot(weights, values, preferred_element_type=F32)
        return 0

    lax.fori_loop(0, (filled + count - 1) // count, attend, 0)
    if not first and not last:

        @pl.when(jnp.logical_not(some))
        def _():
            acc[...] = acc_in[0, 0]

    if last:
        q_most = jnp.max(bound_in[0, 0, 8:16, :])
        safe = jnp.max(most[...]) * q_most <= (SAFE_LOG2 / EXP2_SCALE) ** 2
        for wanted, sums in ((some, acc), (jnp.logical_not(some), acc_in.at[0, 0])):

            @pl.when(safe & wanted)
            def _(sums=sums):
                for h in range(heads):
                    mine = slice(h * rows, (h + 1) * rows)
                    out[:, h * HD : (h + 1) * HD] = (sums[mine, :HD] / sums[mine, HD:]).astype(
                        BF16
                    )

        @pl.when(jnp.logical_not(safe))
        def _():
            def absorb(h, keys, values, shown, fresh):
                mine = pl.ds(pl.multiple_of(h * rows, rows), rows)
                s = jnp.where(shown, scores_of(q_rows[mine, :], keys) * score_scale, masked_score)
                most_now = jnp.max(s, axis=1, keepdims=True)
                if fresh:
                    peak = jnp.broadcast_to(most_now, (rows, HD))
                else:
                    before = peak_ref[mine, :]
                    peak = jnp.maximum(before, most_now)
                w = jnp.where(shown, jnp.exp(s - peak[:, :1]), 0.0)
                total = jnp.broadcast_to(jnp.sum(w, axis=1, keepdims=True), (rows, HD))
                gained = jnp.dot(w.astype(BF16), values, preferred_element_type=F32)
                if not fresh:
                    factor = jnp.exp(before - peak)
                    total = total + total_ref[mine, :] * factor
                    gained = gained + acc[mine, 0:HD] * factor
                peak_ref[mine, :] = peak
                total_ref[mine, :] = total
                acc[mine, 0:HD] = gained

            def own(h, _):
                absorb(h, k_own[...], v_own[...], causal_mask(rows), True)
                return 0

            lax.fori_loop(0, heads, own, 0)
            for p, piece in enumerate(everything):
                base = all_chunks[p](me) * count
                piece = piece.at[slots[p] * count : (slots[p] + 1) * count]

                @pl.when((base < end) & (base + count > start))
                def _(piece=piece, base=base):
                    kcol = pl.multiple_of(kvh * HD, HD)
                    vcol = pl.multiple_of((HALF_KV + kvh) * HD, HD)
                    for col, buf in ((kcol, fetched_k), (vcol, fetched_v)):
                        copy = pltpu.make_async_copy(piece.at[:, pl.ds(col, HD)], buf, sem)
                        copy.start()
                        copy.wait()
                    token = base + lax.broadcasted_iota(jnp.int32, (rows, count), 1)
                    shown = (token >= start) & (token < end)

                    def body(h, _):
                        absorb(h, fetched_k[...], fetched_v[...], shown, False)
                        return 0

                    lax.fori_loop(0, heads, body, 0)

            def finish(h, _):
                mine = pl.ds(pl.multiple_of(h * rows, rows), rows)
                out[:, pl.ds(pl.multiple_of(h * HD, HD), HD)] = (
                    acc[mine, 0:HD] / total_ref[mine, :]
                ).astype(BF16)
                return 0

            lax.fori_loop(0, heads, finish, 0)


def stage(ids, inputs, pieces, state, kept, everything=None, reader=None, whole=False, name="stage"):
    first = state is None
    last = everything is not None
    smem = pl.BlockSpec(memory_space=pltpu.SMEM)
    count = kept["count"]
    rows, heads = kept["rows"], kept["heads"]
    reader0 = reader or 0
    by = lambda k, r: (reader0, k, 0, 0) if last else (r, k, 0, 0)
    place = (lambda k, ids: by(k, 0)) if last else (lambda k, r, ids: by(k, r))
    head = lambda col, part=0: (
        (lambda k, ids: (part, col + k)) if last else (lambda k, r, ids: (part, col + k))
    )
    block = lambda *shape: pl.BlockSpec((1, 1) + shape, place)
    args = [ids]
    specs = []
    for a, spec in inputs:
        args.append(a)
        specs.append(smem if spec is None else spec)
    if not first:
        args += [kept["spans"], kept["q"], kept["k"], kept["v"]]
        specs += [smem, block(heads * rows, HD), block(rows, HD), block(rows, HD)]
    for a, part, _ in pieces:
        args += [a, a]
        specs += [
            pl.BlockSpec((count, HD), head(0, part)),
            pl.BlockSpec((count, HD), head(HALF_KV, part)),
        ]
    acc_spec = block(heads * rows, 2 * HD)
    bound_spec = block(16, HD)
    if not first:
        args += list(state)
        specs += [acc_spec, bound_spec]
    slots = []
    scratch = []
    if last:
        args += [a for a, _, _ in everything]
        specs += [pl.BlockSpec(memory_space=pl.ANY)] * len(everything)
        slots = [part for _, part, _ in everything]
        group = heads * HD
        columns = group * HALF_KV
        if whole:
            out_shape = [jax.ShapeDtypeStruct((rows, 2 * columns), BF16)]
            out_specs = [pl.BlockSpec((rows, group), lambda k, ids: (0, ids[0] * HALF_KV + k))]
        else:
            out_shape = [jax.ShapeDtypeStruct((rows, columns), BF16)]
            out_specs = [pl.BlockSpec((rows, group), lambda k, ids: (0, k))]
        scratch = [
            pltpu.VMEM((heads * rows, 2 * HD), F32),
            pltpu.VMEM((8, HD), F32),
            pltpu.VMEM((count, HD), BF16),
            pltpu.VMEM((count, HD), BF16),
            pltpu.VMEM((heads * rows, HD), F32),
            pltpu.VMEM((heads * rows, HD), F32),
            pltpu.SemaphoreType.DMA,
        ]
    else:
        full = lambda *shape: (2, HALF_KV) + shape
        out_shape = [
            jax.ShapeDtypeStruct(full(heads * rows, 2 * HD), F32),
            jax.ShapeDtypeStruct(full(16, HD), F32),
        ]
        out_specs = [acc_spec, bound_spec]
        if first:
            out_shape += [
                jax.ShapeDtypeStruct((4,), jnp.int32),
                jax.ShapeDtypeStruct(full(heads * rows, HD), BF16),
                jax.ShapeDtypeStruct(full(rows, HD), BF16),
                jax.ShapeDtypeStruct(full(rows, HD), BF16),
            ]
            out_specs += [smem, block(heads * rows, HD), block(rows, HD), block(rows, HD)]
    scratch += [
        pltpu.VMEM(((len(pieces) + 2) * count, HD), BF16),
        pltpu.VMEM(((len(pieces) + 2) * count, 2 * HD), BF16),
    ]
    return pl.pallas_call(
        functools.partial(
            stage_kernel,
            [chunk for _, _, chunk in pieces],
            [chunk for _, _, chunk in everything or ()],
            slots,
            count,
            first,
            last,
            reader0,
        ),
        grid_spec=pltpu.PrefetchScalarGridSpec(
            num_scalar_prefetch=1,
            grid=(HALF_KV,) if last else (HALF_KV, 2),
            in_specs=specs,
            out_specs=out_specs,
            scratch_shapes=scratch,
        ),
        out_shape=out_shape,
        compiler_params=pltpu.CompilerParams(vmem_limit_bytes=VMEM),
        cost_estimate=pl.CostEstimate(
            flops=15000000000 if first else 10000000000,
            bytes_accessed=1 << 18,
            transcendentals=0,
        ),
        name=name,
    )(*args)


def shards(
    prompt_queries,
    prompt_keys,
    prompt_values,
    cache_keys,
    cache_values,
    doc_blocks,
    reader_docs,
    reader_offsets,
):
    size = lax.axis_size("docs")
    me = lax.axis_index("docs").astype(jnp.int32)
    tokens = cache_keys.shape[0]
    half = lax.rem(me, 2)

    def moved(x, pairs):
        return lax.ppermute(
            x, "docs", [(i, j) for i, j in pairs if 0 <= i < size and 0 <= j < size]
        )

    everyone = range(size)
    second = lambda i: (i // 2) % 2
    beside = lambda x: moved(x, [(i, i ^ 1) for i in everyone])
    across = lambda x: moved(x, [(i, i ^ 2) for i in everyone])
    across_other = lambda x: moved(x, [(i, i ^ 3) for i in everyone])
    onward = lambda x: moved(x, [(i, i + 4) for i in everyone])
    onward_other = lambda x: moved(x, [(i, (i + 4) ^ 1) for i in everyone])
    back = lambda x: moved(x, [(i, i - 4) for i in everyone])
    back_other = lambda x: moved(x, [(i, (i - 4) ^ 1) for i in everyone])
    next_other = lambda x: moved(
        x, [(i, (i + 2) ^ 1 if second(i) else (i - 2) ^ 1) for i in everyone]
    )
    relay = lambda x: moved(x, [(i, i - 4 if second(i) else i + 4) for i in everyone])

    rows = prompt_queries.shape[0]
    block_rows = angle_rows(np.arange(COARSE) * BLK, attention_gain)
    coarse_rows = angle_rows(np.arange(COARSE) * COARSE, attention_gain)
    cache_table = np.concatenate(block_rows + angle_rows(np.arange(BLK), 1.0))
    query_table = np.concatenate(coarse_rows + angle_rows(np.arange(rows), 1.0))

    ids = jnp.stack([half, me * (tokens // BLK), me])
    columns = prompt_queries.shape[1] // 2
    width = prompt_keys.shape[1] // 2
    cut = lambda x: lax.dynamic_slice_in_dim(x, (1 - half) * (x.shape[1] // 2), x.shape[1] // 2, 1)
    offset = reader_offsets[0]
    numbers = jnp.stack([reader_docs[0], offset // COARSE, lax.rem(offset, COARSE)])
    numbers = jnp.concatenate([numbers, jnp.zeros((rows // 16 - 3,), jnp.int32)])
    numbers = jnp.broadcast_to(jnp.repeat(numbers.astype(BF16), 16)[:, None], (rows, HD))
    mine, theirs = prepare_cache(
        ids, doc_blocks, jnp.asarray(cache_table), cache_keys, cache_values
    )
    _, prompt_queries, prompt_keys, prompt_values = lax.optimization_barrier(
        (mine, prompt_queries, prompt_keys, prompt_values)
    )
    message = jnp.concatenate(
        [cut(prompt_queries), cut(prompt_keys), cut(prompt_values), numbers], axis=1
    )
    side = beside(message)
    other = beside(theirs)
    across_a = across(mine)
    chip = jnp.concatenate([mine, other], axis=0)
    onward_c = onward(chip)
    back_c = back(chip)
    across_b = across_other(theirs)

    near = [(mine, 0, lambda i: i), (other, 0, lambda i: i ^ 1)]
    group = columns // HALF_KV
    lead = columns // HD
    mine_at = lambda k, r, ids: (0, ids[0] * HALF_KV + k)
    side_at = lambda shift: lambda k, r, ids: (0, shift + k)
    wide = lambda place: pl.BlockSpec((rows, group), place)
    thin = lambda place: pl.BlockSpec((rows, HD), place)
    table = jnp.asarray(query_table)
    inputs = [
        (doc_blocks, None),
        (reader_docs, None),
        (reader_offsets, None),
        (table, pl.BlockSpec(table.shape, lambda k, r, ids: (0, 0))),
        (prompt_queries, wide(mine_at)),
        (prompt_keys, thin(mine_at)),
        (prompt_values, thin(mine_at)),
        (side, wide(side_at(0))),
        (side, thin(side_at(lead))),
        (side, thin(side_at(lead + HALF_KV))),
        (side, thin(lambda k, r, ids: (0, lead + 2 * HALF_KV))),
    ]
    kept = {"count": tokens, "rows": rows, "heads": group // HD}
    acc, bound, spans, turned_q, turned_k, kept_v = stage(
        ids, inputs, near, None, kept, name="near"
    )
    bound, theirs, passing = lax.optimization_barrier((bound, theirs, across_a))
    far_a = relay(passing)
    far_b = next_other(theirs)
    kept.update(spans=spans, q=turned_q, k=turned_k, v=kept_v)
    middle = [
        (onward_c, 0, lambda i: i - 4),
        (onward_c, 1, lambda i: (i - 4) ^ 1),
        (across_a, 0, lambda i: i ^ 2),
        (across_b, 0, lambda i: i ^ 3),
        (back_c, 0, lambda i: i + 4),
        (back_c, 1, lambda i: (i + 4) ^ 1),
    ]
    state = stage(ids, [], middle, (acc, bound), kept, name="middle")

    partner = lambda i: i - 2 + 4 * ((i >> 1) & 1)
    far = [(far_a, 0, partner), (far_b, 0, lambda i: partner(i) ^ 1)]
    everything = near + middle + far
    (side_out,) = stage(ids, [], far, state, kept, everything, 1, name="far_side")
    (own_out,) = stage(ids, [], far, state, kept, everything, 0, True, name="far_own")
    column = (1 - half) * side_out.shape[1]
    return lax.dynamic_update_slice(own_out, beside(side_out), (jnp.int32(0), column))


def solution(mesh):
    both = P(("groups", "docs"))
    wide = P(("groups", "docs"), None)
    placed = (wide, wide, wide, wide, wide, P("groups"), both, both)
    return jax.shard_map(shards, mesh=mesh, in_specs=placed, out_specs=wide, check_vma=False)
```

time: 339 us -> 307 us (0.906)
  Pallas kernels: 308 us -> 279 us
  starting transfers between devices: 18.8 us -> 13.3 us
  other arithmetic: 4.75 us -> 0.73 us
    pallas_call x6 -> x4, Pallas kernels: 304 us -> 276 us  [stage(): pl.pallas_call(functools.partial(stage_kernel, [chunk for _, _, chunk in...]
    ppermute x11 -> x9, starting transfers between devices: 18.8 us -> 13.3 us  [moved(): lax.ppermute(x, 'docs', [(i, j) for i, j in pairs if 0 <= i < size and 0...]
  transfers between devices with their start and end apart: 11 -> 9, of which waited for: 1 -> 1; matrix products, arithmetic and copies ran while one was open for 1% -> 0% of each run, Pallas kernels for 53% -> 52%
where the time goes in v1:
time: 307 us; the launch traced here: 302 us
  Pallas kernels  279 us (91%)
  starting transfers between devices  13.3 us (4%)
  local copies, waits for them, and re-layouts  6.23 us (2%)
    pallas_call x4, Pallas kernels, stage(): pl.pallas_call(functools.partial(stage_kernel, [chunk for _, _, chunk in...  276 us
    ppermute x9, starting transfers between devices, moved(): lax.ppermute(x, 'docs', [(i, j) for i, j in pairs if 0 <= i < size and 0...  13.3 us
  transfers between devices with their start and end apart: 9, of which 1 were waited for; matrix products, arithmetic and copies ran while one was open for 0% of the time, Pallas kernels for 52%

profile of v1, /device:TPU:23, one launch (start us, length us, event | category | flops | bytes accessed | tf_op | source)
XLA Modules:
  0.0 302.1 jit_solution(5179935802382139538)
XLA Ops:
  0.0 0.0 copy-start.3
  0.0 0.0 copy-start.2
  1.4 0.1 pad_maximum_fusion.1
  1.5 0.1 broadcast_in_dim.10
  1.6 0.1 broadcast_in_dim.11
  1.6 0.6 pad_add_fusion.ids.refs_0_
  2.2 3.0 prepare_cache.1
  5.2 0.0 copy-start.7
  5.2 0.0 copy-start
  5.2 1.4 constant_dynamic-slice_fusion.2
  6.6 0.0 copy-done.3
  6.6 0.0 copy-done.2
  6.7 0.1 broadcast_in_dim.12
  6.8 0.1 pad_maximum_fusion
  6.9 0.7 collective-permute-start
  7.6 0.0 copy-done.7
  7.6 0.1 collective-permute-start.1
  7.7 0.5 collective-permute-start.6
  8.2 0.0 copy-done
  8.2 1.3 collective-permute-start.2
  9.5 1.4 collective-permute-done.1.refs_14_.refs_15_.refs_12_
  10.9 0.0 copy-start.1
  10.9 2.1 collective-permute-start.7
  13.0 3.3 %collective-permute-start.5 = (bf16[1024,512]{1,0:T(8,128)(2,1)S(1)}, bf16[1024,512]{1,0:T(8,128)(2,1)S(1)}, u32[]{:S(2)}, u32[]{:S(2)}) collective-permute-start(bf16[1024,512]{1,0:T(8,128)(2,1)S(1)} %constant_dynamic-update-slice_fusion), channel_id=1, source_target_pairs={{0,4},{1,5},{2,6},{3,7},{4,8},{5,9},{6,10},{7,11},{8,12},{9,13},{1... | collective-permute-start | bytes 3145736 | tf_op jit(solution)/shard_map/ppermute | solution.py:484
  16.3 0.0 collective-permute-done.refs_8_.refs_9_.refs_10_.refs_11_
  16.3 0.0 copy-done.1
  16.3 0.0 copy-start.4
  16.3 1.0 copy-done.4
  17.3 20.1 %near.1 = (f32[2,2,2048,256]{3,2,1,0:T(8,128)}, f32[2,2,16,128]{3,2,1,0:T(8,128)}, s32[4]{0:T(128)}, bf16[2,2,2048,128]{3,2,1,0:T(8,128)(2,1)}, bf16[2,2,128,128...) custom-call(s32[3]{0:T(128)} %pad_add_fusion.ids.refs_0_, s32[8]{0:T(128)} %refs_1_.1, s32[1]{0:T(128)S(6)} %copy.13.refs_2_, ...), custom_call_target="tpu_custom_call" | custom-call | flops 15000000512 | bytes 262144 | tf_op jit(solution)/shard_map/near/pallas_call | solution.py:439
  37.4 0.0 collective-permute-done.2.refs_9_.refs_10_.refs_15_
  37.4 0.0 copy-start.9
  37.4 2.0 collective-permute-start.3
  39.5 2.1 collective-permute-start.4
  41.6 0.0 collective-permute-done.6.refs_11_.refs_12_.refs_16_
  41.6 0.0 copy-start.8
  41.6 0.0 collective-permute-done.7.refs_13_.refs_14_.refs_15_.refs_16_.refs_17_.refs_18_
  41.6 0.0 copy-start.5
  41.6 0.0 collective-permute-done.5.refs_5_.refs_6_.refs_7_.refs_8_.refs_13_.refs_14_
  41.6 0.0 copy-start.6
  41.6 0.0 copy-done.9
  41.6 0.8 copy-done.8
  42.4 0.3 copy-done.5
  42.7 0.3 copy-done.6
  43.0 16.3 %middle.1 = (f32[2,2,2048,256]{3,2,1,0:T(8,128)}, f32[2,2,16,128]{3,2,1,0:T(8,128)}) custom-call(s32[3]{0:T(128)} %pad_add_fusion.ids.refs_0_, s32[4]{0:T(128)} %get-tuple-element.26.refs_1_, bf16[2,2,2048,128]{3,2,1,0:T(8,128)(2,1)} %get-tuple-element.27.refs_2_, bf16[2,2,128,128]{3,2,1,0:T(8,128)(2,1)} %get-tuple-element.28.refs_3_, ...), custom_call_target="tpu_custom_call" | custom-call | flops 10000000000 | bytes 262144 | tf_op jit(solution)/shard_map/middle/pallas_call | solution.py:439
  59.4 0.0 collective-permute-done.3.refs_5_.refs_6_.refs_19_
  59.4 0.0 copy-start.10
  59.4 0.0 collective-permute-done.4.refs_7_.refs_8_.refs_20_
  59.4 0.0 copy-start.11
  59.4 0.8 copy-done.10
  60.2 0.2 copy-done.11
  60.4 119.7 %far_side.1 = bf16[128,4096]{1,0:T(8,128)(2,1)} custom-call(s32[3]{0:T(128)} %pad_add_fusion.ids.refs_0_, s32[4]{0:T(128)} %get-tuple-element.26.refs_1_, bf16[2,2,2048,128]{3,2,1,0:T(8,128)(2,1)} %get-tuple-element.27.refs_2_, bf16[2,2,128,128]{3,2,1,0:T(8,128)(2,1)} %get-tuple-element.28.refs_3_, bf16[2,2,128,128]{3,2,1,0:T(8,128)(2,1)} %get-tuple-element.29.refs_4_, ...), custom_call_target="tpu_custom_call" | custom-call | flops 10000000000 | bytes 262144 | tf_op jit(solution)/shard_map/far_side/pallas_call | solution.py:439
  180.1 1.3 collective-permute-start.8
  181.3 119.6 %far_own.1 = bf16[128,8192]{1,0:T(8,128)(2,1)} custom-call(s32[3]{0:T(128)} %pad_add_fusion.ids.refs_0_, s32[4]{0:T(128)} %get-tuple-element.26.refs_1_, bf16[2,2,2048,128]{3,2,1,0:T(8,128)(2,1)} %get-tuple-element.27.refs_2_, bf16[2,2,128,128]{3,2,1,0:T(8,128)(2,1)} %get-tuple-element.28.refs_3_, bf16[2,2,128,128]{3,2,1,0:T(8,128)(2,1)} %get-tuple-element.29.refs_4_, ...), custom_call_target="tpu_custom_call" | custom-call | flops 10000000000 | bytes 262144 | tf_op jit(solution)/shard_map/far_own/pallas_call | solution.py:439
  301.0 0.0 collective-permute-done.8
  301.0 1.1 constant_dynamic-update-slice_fusion.2
  (4 shorter events, 0.1 us)
Async XLA Ops:
  0.0 6.6 %copy-start.3 = (bf16[128,512]{1,0:T(8,128)(2,1)S(1)}, bf16[128,512]{1,0:T(8,128)(2,1)}, u32[]{:S(2)}) copy-start(bf16[128,512]{1,0:T(8,128)(2,1)} %refs_7_) | copy-start | bytes 393220
  0.0 6.6 %copy-start.2 = (bf16[128,512]{1,0:T(8,128)(2,1)S(1)}, bf16[128,512]{1,0:T(8,128)(2,1)}, u32[]{:S(2)}) copy-start(bf16[128,512]{1,0:T(8,128)(2,1)} %refs_6_) | copy-start | bytes 393220
  5.2 2.4 copy-start.7
  5.2 3.0 copy-start
  6.9 9.4 %collective-permute-start = (bf16[128,4736]{1,0:T(8,128)(2,1)S(1)}, bf16[128,4736]{1,0:T(8,128)(2,1)S(1)}, u32[]{:S(2)}, u32[]{:S(2)}) collective-permute-start(bf16[128,4736]{1,0:T(8,128)(2,1)S(1)} %pad_maximum_fusion), channel_id=1, source_target_pairs={{0,1},{1,0},{2,3},{3,2},{4,5},{5,4},{6,7},{7,6},{8,9},{9,8},{10,11... | collective-permute-start | bytes 3637256 | tf_op jit(solution)/shard_map/ppermute | solution.py:484
  7.6 3.3 %collective-permute-start.1 = (bf16[512,512]{1,0:T(8,128)(2,1)S(1)}, bf16[512,512]{1,0:T(8,128)(2,1)S(1)}, u32[]{:S(2)}, u32[]{:S(2)}) collective-permute-start(bf16[512,512]{1,0:T(8,128)(2,1)S(1)} %copy-done.7), channel_id=1, source_target_pairs={{0,1},{1,0},{2,3},{3,2},{4,5},{5,4},{6,7},{7,6},{8,9},{9,8},{10,11... | collective-permute-start | bytes 1572872 | tf_op jit(solution)/shard_map/ppermute | solution.py:484
  7.7 33.9 %collective-permute-start.6 = (bf16[512,512]{1,0:T(8,128)(2,1)S(1)}, bf16[512,512]{1,0:T(8,128)(2,1)S(1)}, u32[]{:S(2)}, u32[]{:S(2)}) collective-permute-start(bf16[512,512]{1,0:T(8,128)(2,1)S(1)} %copy-done.7), channel_id=1, source_target_pairs={{0,3},{1,2},{2,1},{3,0},{4,7},{5,6},{6,5},{7,4},{8,11},{9,10},{10,... | collective-permute-start | bytes 1572872 | tf_op jit(solution)/shard_map/ppermute | solution.py:484
  8.2 29.2 %collective-permute-start.2 = (bf16[512,512]{1,0:T(8,128)(2,1)S(1)}, bf16[512,512]{1,0:T(8,128)(2,1)S(1)}, u32[]{:S(2)}, u32[]{:S(2)}) collective-permute-start(bf16[512,512]{1,0:T(8,128)(2,1)S(1)} %copy-done), channel_id=1, source_target_pairs={{0,2},{1,3},{2,0},{3,1},{4,6},{5,7},{6,4},{7,5},{8,10},{9,11},{10,... | collective-permute-start | bytes 1572872 | tf_op jit(solution)/shard_map/ppermute | solution.py:484
  10.9 5.4 %copy-start.1 = (bf16[512,512]{1,0:T(8,128)(2,1)}, bf16[512,512]{1,0:T(8,128)(2,1)S(1)}, u32[]{:S(2)}) copy-start(bf16[512,512]{1,0:T(8,128)(2,1)S(1)} %collective-permute-done.1.refs_14_.refs_15_.refs_12_) | copy-start | bytes 1572868
  10.9 30.7 %collective-permute-start.7 = (bf16[1024,512]{1,0:T(8,128)(2,1)S(1)}, bf16[1024,512]{1,0:T(8,128)(2,1)S(1)}, u32[]{:S(2)}, u32[]{:S(2)}) collective-permute-start(bf16[1024,512]{1,0:T(8,128)(2,1)S(1)} %constant_dynamic-update-slice_fusion), channel_id=1, source_target_pairs={{4,0},{5,1},{6,2},{7,3},{8,4},{9,5},{10,6},{11,7},{12,8},{13,9},{1... | collective-permute-start | bytes 3145736 | tf_op jit(solution)/shard_map/ppermute | solution.py:484
  13.0 28.6 %collective-permute-start.5 = (bf16[1024,512]{1,0:T(8,128)(2,1)S(1)}, bf16[1024,512]{1,0:T(8,128)(2,1)S(1)}, u32[]{:S(2)}, u32[]{:S(2)}) collective-permute-start(bf16[1024,512]{1,0:T(8,128)(2,1)S(1)} %constant_dynamic-update-slice_fusion), channel_id=1, source_target_pairs={{0,4},{1,5},{2,6},{3,7},{4,8},{5,9},{6,10},{7,11},{8,12},{9,13},{1... | collective-permute-start | bytes 3145736 | tf_op jit(solution)/shard_map/ppermute | solution.py:484
  16.3 1.0 copy-start.4
  37.4 4.2 %copy-start.9 = (bf16[512,512]{1,0:T(8,128)(2,1)}, bf16[512,512]{1,0:T(8,128)(2,1)S(1)}, u32[]{:S(2)}) copy-start(bf16[512,512]{1,0:T(8,128)(2,1)S(1)} %collective-permute-done.2.refs_9_.refs_10_.refs_15_) | copy-start | bytes 1572868
  37.4 22.0 %collective-permute-start.3 = (bf16[512,512]{1,0:T(8,128)(2,1)S(1)}, bf16[512,512]{1,0:T(8,128)(2,1)S(1)}, u32[]{:S(2)}, u32[]{:S(2)}) collective-permute-start(bf16[512,512]{1,0:T(8,128)(2,1)S(1)} %collective-permute-done.2.refs_9_.refs_10_.refs_15_), channel_id=1, source_target_pairs={{0,4},{1,5},{4,8},{5,9},{6,2},{7,3},{8,12},{9,13},{10,6},{11,7},{1... | collective-permute-start | bytes 1572872 | tf_op jit(solution)/shard_map/ppermute | solution.py:484
  39.5 19.9 %collective-permute-start.4 = (bf16[512,512]{1,0:T(8,128)(2,1)S(1)}, bf16[512,512]{1,0:T(8,128)(2,1)S(1)}, u32[]{:S(2)}, u32[]{:S(2)}) collective-permute-start(bf16[512,512]{1,0:T(8,128)(2,1)S(1)} %copy-done.7), channel_id=1, source_target_pairs={{2,5},{3,4},{4,3},{5,2},{6,9},{7,8},{8,7},{9,6},{10,13},{11,12},{1... | collective-permute-start | bytes 1572872 | tf_op jit(solution)/shard_map/ppermute | solution.py:484
  41.6 0.8 copy-start.8
  41.6 1.1 copy-start.5
  41.6 1.4 copy-start.6
  59.4 0.8 copy-start.10
  59.4 1.0 copy-start.11
  180.1 120.9 %collective-permute-start.8 = (bf16[128,4096]{1,0:T(8,128)(2,1)}, bf16[128,4096]{1,0:T(8,128)(2,1)S(1)}, u32[]{:S(2)}, u32[]{:S(2)}) collective-permute-start(bf16[128,4096]{1,0:T(8,128)(2,1)} %far_side.1), channel_id=1, source_target_pairs={{0,1},{1,0},{2,3},{3,2},{4,5},{5,4},{6,7},{7,6},{8,9},{9,8},{10,11... | collective-permute-start | bytes 3145736 | tf_op jit(solution)/shard_map/ppermute | solution.py:484
